TPU v7x, 256 devices: a whole 4x4x8 slice. The times are simulated.
256 devices in a mesh: row: 2 (over y_lo), col: 128 (over x, y_hi, z, core).
Axes of the slice: x: 4, y: 4 (y_hi: 2, y_lo: 2; y = y_hi * 2 + y_lo), z: 8, core: 2. Of those that a mesh axis runs over, the one named last changes fastest.
Arguments:
- slab: bfloat16 [8192, 131072], P('row', 'col'), may hold values from -0.0625 to 0.0625
- tones: bfloat16 [131072, 64], P('col', 'row'), may hold values from -6 to 6
Outputs:
- images: float32 [8192, 64], P(('row', 'col'))
All inputs are finite; a program needn't handle non-finite values.
Results may differ from a plain program's by a relative error of at most 0.0003.
Values may be sent and summed in bfloat16 or wider, within the bound.
No kernel may reach another device: no remote copies, remote signals or barrier semaphores. Data moves between devices by JAX's collectives and lax.ppermute only.
A program may use at most 64 MiB of HBM per device.

v0:
```python
import jax
import jax.numpy as jnp
from jax import lax
from jax.sharding import PartitionSpec as P


def shards(slab, tones):
    vectors = lax.all_gather(tones, "row", axis=1, tiled=True)
    partial_value = jnp.dot(slab, vectors, preferred_element_type=jnp.float32)
    images = lax.psum_scatter(partial_value, "col", scatter_dimension=0, tiled=True)
    return images


def solution(mesh):
    placed = (P("row", "col"), P("col", "row"))
    return jax.shard_map(
        shards, mesh=mesh, in_specs=placed, out_specs=P(("row", "col"), None), check_vma=False
    )
```

profile of v0, /device:TPU:8, one launch (start us, length us, event | category | flops | bytes accessed | tf_op | source)
XLA Modules:
  0.0 688.5 jit_solution(2921881493178899184)
XLA Ops:
  6.5 0.0 reduce-scatter.2.cloned.1.call-start
  6.5 5.3 all_gather.3
  11.9 7.1 %fusion = f32[4096,64]{1,0:T(8,128)} fusion(bf16[4096,1024]{1,0:T(8,128)(2,1)} %param.2, bf16[1024,64]{0,1:T(8,128)(2,1)S(1)} %all_gather.3), kind=kOutput, calls=%fused_computation | convolution fusion | flops 536870912 | bytes 9568256 | tf_op jit(solution)/shard_map/dot_general | solution.py:9
  18.9 0.0 reduce-scatter.2.cloned.1.call-update
  19.0 662.7 %reduce-scatter.2.cloned.1.call-done = f32[32,64]{1,0:T(8,128)} async-done(((f32[4096,64]{1,0:T(8,128)}), f32[32,64]{1,0:T(8,128)}) %reduce-scatter.2.cloned.1.call-update) | async-done | bytes 8208 | tf_op jit(solution)/shard_map/reduce_scatter | solution.py:10
Async XLA Ops:
  6.5 675.1 %reduce-scatter.2.cloned.1.call-start = ((), (), s32[]{:S(2)}) async-start(), calls=%async_computation.1 | async-start | bytes 2113536 | tf_op jit(solution)/shard_map/reduce_scatter | solution.py:10
Sparse Core Ops, SparseCore 0:
  19.1 662.5 reduce-scatter.1
where the time goes:
time: 689 us; the launch traced here: 688 us
  waiting for transfers between devices  663 us (96%)
  between operations  13.4 us (2%)
  matrix products  7.06 us (1%)
    reduce_scatter x1, waiting for transfers between devices, shards(): lax.psum_scatter(partial_value, 'col', scatter_dimension=0, tiled=True)  663 us
  transfers between devices with their start and end apart: 1, of which 1 were waited for; matrix products, arithmetic and copies ran while one was open for 0% of the time, Pallas kernels for 0%

commit v1 on v0

v1 whole, which is shorter than its diff:
```python
import functools

import jax
import jax.numpy as jnp
from jax import lax
from jax.experimental import pallas as pl
from jax.experimental.pallas import tpu as pltpu
from jax.sharding import PartitionSpec as P

CHIPS = 64
LANES = 128
PIECES = 8


def load_kernel(slab_ref, held_ref, sems):
    size = slab_ref.shape[0] // PIECES
    copies = [
        pltpu.make_async_copy(
            slab_ref.at[pl.ds(piece * size, size)],
            held_ref.at[pl.ds(piece * size, size)],
            sems.at[piece],
        )
        for piece in range(PIECES)
    ]
    for copy in copies:
        copy.start()
    for copy in copies:
        copy.wait()


def load(slab):
    return pl.pallas_call(
        load_kernel,
        in_specs=[pl.BlockSpec(memory_space=pltpu.HBM)],
        out_specs=pl.BlockSpec(memory_space=pl.ANY),
        out_shape=pltpu.VMEM(slab.shape, slab.dtype),
        scratch_shapes=[pltpu.SemaphoreType.DMA((PIECES,))],
        compiler_params=pltpu.CompilerParams(vmem_limit_bytes=2**20),
        cost_estimate=pl.CostEstimate(flops=0, bytes_accessed=2 * slab.size * 2, transcendentals=0),
    )(slab)


def product_kernel(flip, slab_ref, near_ref, far_ref, out_ref, weights):
    chips, _, _, half, depth = slab_ref.shape
    nvec = near_ref.shape[0]
    which = (lax.axis_index("col") + flip) & 1
    row = lax.axis_index("row")
    near = pl.multiple_of(row * nvec, nvec)
    far = pl.multiple_of((1 - row) * nvec, nvec)
    weights[...] = jnp.zeros_like(weights)
    for part in range(2):
        weights[part, pl.ds(2 * nvec * part + near, nvec), :] = near_ref[...]
        weights[part, pl.ds(2 * nvec * part + far, nvec), :] = far_ref[...]
    contract = (((1,), (1,)), ((), ()))
    steps = 1
    block = chips // steps

    @pl.loop(0, steps)
    def _(step):
        at = pl.ds(step * block, block)
        top = slab_ref[at, which, 0].reshape(block * half, depth)
        low = slab_ref[at, which, 1].reshape(block * half, depth)
        rows = pl.ds(pl.multiple_of(step * block * half, block * half), block * half)
        out_ref[rows, :] = lax.dot_general(
            top, weights[0], contract, preferred_element_type=jnp.float32
        ) + lax.dot_general(
            low, weights[1], contract, preferred_element_type=jnp.float32
        )


def product(flip, slab, near, far):
    chips, _, _, half, depth = slab.shape
    nvec = near.shape[0]
    return pl.pallas_call(
        functools.partial(product_kernel, flip),
        in_specs=[
            pl.BlockSpec(memory_space=pltpu.VMEM),
            pl.BlockSpec(memory_space=pltpu.VMEM),
            pl.BlockSpec(memory_space=pltpu.VMEM),
        ],
        out_specs=pl.BlockSpec(memory_space=pltpu.VMEM),
        scratch_shapes=[pltpu.VMEM((2, 4 * nvec, depth), slab.dtype)],
        out_shape=pltpu.VMEM((chips * half, LANES), jnp.float32),
        compiler_params=pltpu.CompilerParams(vmem_limit_bytes=30 * 2**20),
        cost_estimate=pl.CostEstimate(
            flops=2 * chips * 2 * half * depth * nvec * 2,
            bytes_accessed=chips * 2 * half * depth * 2,
            transcendentals=0,
        ),
    )(slab, near, far)


def total_kernel(parts_ref, out_ref):
    half, lanes = parts_ref.shape[1:]
    total = jnp.sum(parts_ref[...], axis=0)
    out_ref[0:half, :] = total[:, 0 : lanes // 2]
    out_ref[half:, :] = total[:, lanes // 2 :]


def shards(slab, tones):
    rows, depth = slab.shape
    half = rows // CHIPS // 4
    near = tones.T
    far = lax.ppermute(near, "row", [(0, 1), (1, 0)])
    held = load(slab.reshape(CHIPS, 2, 2, half, depth))
    other = product(1, held, near, far)
    mine = product(0, held, near, far)
    pairs = [(i, i ^ 1) for i in range(2 * CHIPS)]
    mine = mine + lax.ppermute(other, "col", pairs)
    groups = [[2 * chip + core for chip in range(CHIPS)] for core in range(2)]
    parts = lax.all_to_all(mine, "col", 0, 0, axis_index_groups=groups, tiled=True)
    return pl.pallas_call(
        total_kernel,
        out_shape=jax.ShapeDtypeStruct((2 * half, LANES // 2), jnp.float32),
        compiler_params=pltpu.CompilerParams(vmem_limit_bytes=4 * 2**20),
    )(parts.reshape(CHIPS, half, LANES))


def solution(mesh):
    placed = (P("row", "col"), P("col", "row"))
    return jax.shard_map(
        shards, mesh=mesh, in_specs=placed, out_specs=P(("row", "col"), None), check_vma=False
    )
```

time: 689 us -> 44 us (0.06)
  the two profiles are of different devices: /device:TPU:8 before, /device:TPU:32 now
where the time goes in v1:
time: 44 us; the launch traced here: 43.8 us
  blocking collectives  33.9 us (77%)
  Pallas kernels  3.95 us (9%)
  local copies, waits for them, and re-layouts  3.56 us (8%)
  starting transfers between devices  1.67 us (4%)
  waiting for transfers between devices  0.62 us (1%)
    all_to_all x1, blocking collectives, shards(): lax.all_to_all(mine, 'col', 0, 0, axis_index_groups=groups, tiled=True)  33.9 us
    unnamed x4, local copies, waits for them, and re-layouts  3.56 us
    pallas_call x2, Pallas kernels, product(): pl.pallas_call(functools.partial(product_kernel, flip), in_specs=[pl.Bloc...  2.56 us
    ppermute x1, starting transfers between devices, shards(): far = lax.ppermute(near, 'row', [(0, 1), (1, 0)])  1.58 us
  transfers between devices with their start and end apart: 2, of which 1 were waited for; matrix products, arithmetic and copies ran while one was open for 0% of the time, Pallas kernels for 4%

profile of v1, /device:TPU:32, one launch (start us, length us, event | category | flops | bytes accessed | tf_op | source)
XLA Modules:
  0.0 43.8 jit_solution(1275747304823291226)
XLA Ops:
  0.0 1.6 %collective-permute-start = (bf16[32,1024]{1,0:T(8,128)(2,1)}, bf16[32,1024]{1,0:T(8,128)(2,1)S(1)}, u32[]{:S(2)}, u32[]{:S(2)}) collective-permute-start(bf16[32,1024]{1,0:T(8,128)(2,1)} %bitcast.4), channel_id=1, source_target_pairs={{0,128},{128,0},{1,129},{129,1},{2,130},{130,2},{3,131},{131,3},{4... | collective-permute-start | bytes 196616 | tf_op jit(solution)/shard_map/ppermute | solution.py:104
  1.6 0.0 copy-start
  1.6 3.4 %copy-done = bf16[4096,1024]{1,0:T(8,128)(2,1)S(1)} copy-done((bf16[4096,1024]{1,0:T(8,128)(2,1)S(1)}, bf16[4096,1024]{1,0:T(8,128)(2,1)}, u32[]{:S(2)}) %copy-start) | copy-done | bytes 8388632
  5.0 0.0 copy-start.1
  5.0 0.6 %shard_map.28.slab_ref = bf16[64,2,2,16,1024]{4,3,2,1,0:T(8,128)(2,1)S(1)} custom-call(bf16[64,2,2,16,1024]{4,3,2,1,0:T(8,128)(2,1)S(1)} %bitcast.3), custom_call_target="tpu_custom_call" | custom-call | bytes 16777216 | tf_op jit(solution)/shard_map/pallas_call | solution.py:32
  5.6 0.0 collective-permute-done.far_ref
  5.6 0.2 copy-done.1
  5.8 1.3 %shard_map.30 = f32[1024,128]{1,0:T(8,128)S(1)} custom-call(bf16[64,2,2,16,1024]{4,3,2,1,0:T(8,128)(2,1)S(1)} %shard_map.28.slab_ref, bf16[32,1024]{1,0:T(8,128)(2,1)S(1)} %bitcast.5, bf16[32,1024]{1,0:T(8,128)(2,1)S(1)} %collective-permute-done.far_ref), custom_call_target="tpu_custom_call" | custom-call | flops 268435456 | bytes 4194304 | tf_op jit(solution)/shard_map/pallas_call | solution.py:74
  7.1 0.1 collective-permute-start.1
  7.2 1.3 %shard_map.29 = f32[1024,128]{1,0:T(8,128)S(1)} custom-call(bf16[64,2,2,16,1024]{4,3,2,1,0:T(8,128)(2,1)S(1)} %shard_map.28.slab_ref, bf16[32,1024]{1,0:T(8,128)(2,1)S(1)} %bitcast.6, bf16[32,1024]{1,0:T(8,128)(2,1)S(1)} %collective-permute-done.far_ref), custom_call_target="tpu_custom_call" | custom-call | flops 268435456 | bytes 4194304 | tf_op jit(solution)/shard_map/pallas_call | solution.py:74
  8.5 0.6 %collective-permute-done.1 = f32[1024,128]{1,0:T(8,128)S(1)} collective-permute-done((f32[1024,128]{1,0:T(8,128)S(1)}, f32[1024,128]{1,0:T(8,128)S(1)}, u32[]{:S(2)}, u32[]{:S(2)}) %collective-permute-start.1) | collective-permute-done | bytes 524320 | tf_op jit(solution)/shard_map/ppermute | solution.py:109
  9.1 0.1 add.3
  9.1 33.9 %all_to_all.9.parts_ref = f32[64,16,128]{2,1,0:T(8,128)S(1)} all-to-all(f32[64,16,128]{2,1,0:T(8,128)S(1)} %bitcast.7), channel_id=1, replica_groups={{0,2,4,6,8,10,12,14,16,18,20,22,24,26,28,30,32,34,36,38,40,42,44,46,48,..., dimensions={0} | all-to-all | bytes 1048576 | tf_op jit(solution)/shard_map/all_to_all | solution.py:111
  43.0 0.7 %shard_map.31 = f32[32,64]{1,0:T(8,128)} custom-call(f32[64,16,128]{2,1,0:T(8,128)S(1)} %all_to_all.9.parts_ref), custom_call_target="tpu_custom_call" | custom-call | tf_op jit(solution)/shard_map/pallas_call | solution.py:112
Async XLA Ops:
  0.0 5.6 %collective-permute-start = (bf16[32,1024]{1,0:T(8,128)(2,1)}, bf16[32,1024]{1,0:T(8,128)(2,1)S(1)}, u32[]{:S(2)}, u32[]{:S(2)}) collective-permute-start(bf16[32,1024]{1,0:T(8,128)(2,1)} %bitcast.4), channel_id=1, source_target_pairs={{0,128},{128,0},{1,129},{129,1},{2,130},{130,2},{3,131},{131,3},{4... | collective-permute-start | bytes 196616 | tf_op jit(solution)/shard_map/ppermute | solution.py:104
  1.6 3.4 %copy-start = (bf16[4096,1024]{1,0:T(8,128)(2,1)S(1)}, bf16[4096,1024]{1,0:T(8,128)(2,1)}, u32[]{:S(2)}) copy-start(bf16[4096,1024]{1,0:T(8,128)(2,1)} %param.2) | copy-start | bytes 25165828
  5.0 0.8 %copy-start.1 = (bf16[1024,32]{0,1:T(8,128)(2,1)S(1)}, bf16[1024,32]{0,1:T(8,128)(2,1)}, u32[]{:S(2)}) copy-start(bf16[1024,32]{0,1:T(8,128)(2,1)} %param.3) | copy-start | bytes 196612
  7.1 2.0 %collective-permute-start.1 = (f32[1024,128]{1,0:T(8,128)S(1)}, f32[1024,128]{1,0:T(8,128)S(1)}, u32[]{:S(2)}, u32[]{:S(2)}) collective-permute-start(f32[1024,128]{1,0:T(8,128)S(1)} %shard_map.30), channel_id=1, source_target_pairs={{0,1},{1,0},{2,3},{3,2},{4,5},{5,4},{6,7},{7,6},{8,9},{9,8},{10,11... | collective-permute-start | bytes 1572872 | tf_op jit(solution)/shard_map/ppermute | solution.py:109

commit v2 on v0

v2 whole, which is shorter than its diff:
```python
import functools

import jax
import jax.numpy as jnp
from jax import lax
from jax.experimental import pallas as pl
from jax.experimental.pallas import tpu as pltpu
from jax.sharding import PartitionSpec as P

PLANES = 8
CHIPS = 64
LANES = 128


def load_kernel(slab_ref, held_ref, sems):
    copies = [
        pltpu.make_async_copy(slab_ref.at[piece], held_ref.at[piece], sems.at[piece])
        for piece in range(slab_ref.shape[0])
    ]
    for copy in copies:
        copy.start()
    for copy in copies:
        copy.wait()


def load(slab):
    return pl.pallas_call(
        load_kernel,
        in_specs=[pl.BlockSpec(memory_space=pltpu.HBM)],
        out_specs=pl.BlockSpec(memory_space=pltpu.VMEM),
        out_shape=pltpu.VMEM(slab.shape, slab.dtype),
        scratch_shapes=[pltpu.SemaphoreType.DMA((slab.shape[0],))],
        compiler_params=pltpu.CompilerParams(vmem_limit_bytes=2**24),
        cost_estimate=pl.CostEstimate(flops=0, bytes_accessed=4 * slab.size, transcendentals=0),
    )(slab)


def fill(weights, near_ref, far_ref):
    nvec = near_ref.shape[0]
    row = lax.axis_index("row")
    near = pl.multiple_of(row * nvec, nvec)
    far = pl.multiple_of((1 - row) * nvec, nvec)
    zero = jnp.zeros((2 * nvec, weights.shape[2]), weights.dtype)
    for part in range(2):
        weights[part, pl.ds(2 * nvec * part + near, nvec), :] = near_ref[...]
        weights[part, pl.ds(2 * nvec * part + far, nvec), :] = far_ref[...]
        weights[part, pl.ds(2 * nvec * (1 - part), 2 * nvec), :] = zero


def multiply(slab_ref, which, weights, out_ref):
    planes, half, depth = slab_ref.shape[1], slab_ref.shape[4], slab_ref.shape[5]
    contract = (((1,), (1,)), ((), ()))
    total = None
    for part in range(2):
        rows = jnp.concatenate(
            [slab_ref[:, z, which, part].reshape(-1, depth) for z in range(planes)]
        )
        term = lax.dot_general(rows, weights[part], contract, preferred_element_type=jnp.float32)
        total = term if total is None else total + term
    out_ref[...] = total


def first_kernel(slab_ref, near_ref, far_ref, out_ref, weights):
    fill(weights, near_ref, far_ref)
    multiply(slab_ref, 1 - (lax.axis_index("col") & 1), weights, out_ref)


def second_kernel(slab_ref, weights, out_ref):
    multiply(slab_ref, lax.axis_index("col") & 1, weights, out_ref)


VM = pl.BlockSpec(memory_space=pltpu.VMEM)


def total_kernel(parts_ref, out_ref):
    half, lanes = parts_ref.shape[1:]
    total = jnp.sum(parts_ref[...], axis=0)
    out_ref[0:half, :] = total[:, 0 : lanes // 2]
    out_ref[half:, :] = total[:, lanes // 2 :]


def shards(slab, tones):
    rows, depth = slab.shape
    nvec = tones.shape[1]
    half = rows // CHIPS // 4
    near = tones.T
    far = lax.ppermute(near, "row", [(0, 1), (1, 0)])
    slab = slab.reshape(CHIPS // PLANES, PLANES, 2, 2, half, depth)
    cost = pl.CostEstimate(flops=rows * depth * nvec * 2, bytes_accessed=rows * depth, transcendentals=0)
    product = pltpu.VMEM((CHIPS * half, LANES), jnp.float32)
    held = load(pltpu.with_memory_space_constraint(slab, pltpu.HBM))
    other, weights = pl.pallas_call(
        first_kernel,
        in_specs=[VM] * 3,
        out_specs=[VM, VM],
        out_shape=[product, pltpu.VMEM((2, LANES, depth), slab.dtype)],
        compiler_params=pltpu.CompilerParams(vmem_limit_bytes=30 * 2**20),
        cost_estimate=cost,
    )(held, near, far)
    mine = pl.pallas_call(
        second_kernel,
        in_specs=[VM] * 2,
        out_specs=VM,
        out_shape=product,
        compiler_params=pltpu.CompilerParams(vmem_limit_bytes=30 * 2**20),
        cost_estimate=cost,
    )(held, weights)
    pairs = [(i, i ^ 1) for i in range(2 * CHIPS)]
    mine = mine + lax.ppermute(other, "col", pairs)
    across = CHIPS // PLANES
    order = [xy * PLANES + z for z in range(PLANES) for xy in range(across)]
    groups = [[2 * chip + core for chip in order] for core in range(2)]
    parts = lax.all_to_all(mine, "col", 0, 0, axis_index_groups=groups, tiled=True)
    return pl.pallas_call(
        total_kernel,
        out_shape=jax.ShapeDtypeStruct((2 * half, LANES // 2), jnp.float32),
        compiler_params=pltpu.CompilerParams(vmem_limit_bytes=4 * 2**20),
    )(parts.reshape(CHIPS, half, LANES))


def solution(mesh):
    placed = (P("row", "col"), P("col", "row"))
    return jax.shard_map(
        shards, mesh=mesh, in_specs=placed, out_specs=P(("row", "col"), None), check_vma=False
    )
```

time: 689 us -> 42.5 us (0.06)
  the two profiles are of different devices: /device:TPU:8 before, /device:TPU:4 now
where the time goes in v2:
time: 42.5 us; the launch traced here: 41.8 us
  blocking collectives  32.6 us (77%)
  Pallas kernels  6.76 us (16%)
  starting transfers between devices  1.67 us (4%)
  waiting for transfers between devices  0.64 us (2%)
    all_to_all x1, blocking collectives, shards(): lax.all_to_all(mine, 'col', 0, 0, axis_index_groups=groups, tiled=True)  32.6 us
    pallas_call x1, Pallas kernels, load(): pl.pallas_call(load_kernel, in_specs=[pl.BlockSpec(memory_space=pltpu.HBM...  3.5 us
    ppermute x1, starting transfers between devices, shards(): far = lax.ppermute(near, 'row', [(0, 1), (1, 0)])  1.58 us
    pallas_call x1, Pallas kernels, shards(): pl.pallas_call(first_kernel, in_specs=[VM] * 3, out_specs=[VM, VM], out_s...  1.27 us
    pallas_call x1, Pallas kernels, shards(): pl.pallas_call(second_kernel, in_specs=[VM] * 2, out_specs=VM, out_shape=...  1.25 us
  transfers between devices with their start and end apart: 2, of which 1 were waited for; matrix products, arithmetic and copies ran while one was open for 0% of the time, Pallas kernels for 11%

profile of v2, /device:TPU:4, one launch (start us, length us, event | category | flops | bytes accessed | tf_op | source)
XLA Modules:
  0.0 41.8 jit_solution(11525347900484726149)
XLA Ops:
  0.0 1.6 %collective-permute-start = (bf16[32,1024]{1,0:T(8,128)(2,1)}, bf16[32,1024]{1,0:T(8,128)(2,1)S(1)}, u32[]{:S(2)}, u32[]{:S(2)}) collective-permute-start(bf16[32,1024]{1,0:T(8,128)(2,1)} %bitcast.3), channel_id=1, source_target_pairs={{0,128},{128,0},{1,129},{129,1},{2,130},{130,2},{3,131},{131,3},{4... | collective-permute-start | bytes 196616 | tf_op jit(solution)/shard_map/ppermute | solution.py:87
  1.6 0.0 copy-start
  1.6 3.5 %shard_map.28.slab_ref = bf16[8,8,2,2,16,1024]{5,4,3,2,1,0:T(8,128)(2,1)S(1)} custom-call(bf16[8,8,2,2,16,1024]{5,4,3,2,1,0:T(8,128)(2,1)} %bitcast.5), custom_call_target="tpu_custom_call" | custom-call | bytes 16777216 | tf_op jit(solution)/shard_map/pallas_call | solution.py:27
  5.1 0.0 collective-permute-done.far_ref
  5.1 0.0 copy-done
  5.1 1.3 %shard_map.29 = (f32[1024,128]{1,0:T(8,128)S(1)}, bf16[2,128,1024]{2,1,0:T(8,128)(2,1)S(1)}) custom-call(bf16[8,8,2,2,16,1024]{5,4,3,2,1,0:T(8,128)(2,1)S(1)} %shard_map.28.slab_ref, bf16[32,1024]{1,0:T(8,128)(2,1)S(1)} %bitcast.4, bf16[32,1024]{1,0:T(8,128)(2,1)S(1)} %collective-permute-done.far_ref), custom_call_target="tpu_custom_call" | custom-call | flops 268435456 | bytes 4194304 | tf_op jit(solution)/shard_map/pallas_call | solution.py:92
  6.4 0.1 collective-permute-start.1
  6.5 1.2 %shard_map.30 = f32[1024,128]{1,0:T(8,128)S(1)} custom-call(bf16[8,8,2,2,16,1024]{5,4,3,2,1,0:T(8,128)(2,1)S(1)} %shard_map.28.slab_ref, bf16[2,128,1024]{2,1,0:T(8,128)(2,1)S(1)} %get-tuple-element.7.weights), custom_call_target="tpu_custom_call" | custom-call | flops 268435456 | bytes 4194304 | tf_op jit(solution)/shard_map/pallas_call | solution.py:100
  7.7 0.6 %collective-permute-done.1 = f32[1024,128]{1,0:T(8,128)S(1)} collective-permute-done((f32[1024,128]{1,0:T(8,128)S(1)}, f32[1024,128]{1,0:T(8,128)S(1)}, u32[]{:S(2)}, u32[]{:S(2)}) %collective-permute-start.1) | collective-permute-done | bytes 524320 | tf_op jit(solution)/shard_map/ppermute | solution.py:109
  8.4 0.1 add.3
  8.4 32.6 %all_to_all.9.parts_ref = f32[64,16,128]{2,1,0:T(8,128)S(1)} all-to-all(f32[64,16,128]{2,1,0:T(8,128)S(1)} %bitcast.6), channel_id=1, replica_groups={{0,16,32,48,64,80,96,112,2,18,34,50,66,82,98,114,4,20,36,52,68,84,100,1..., dimensions={0} | all-to-all | bytes 1048576 | tf_op jit(solution)/shard_map/all_to_all | solution.py:113
  41.0 0.7 %shard_map.31 = f32[32,64]{1,0:T(8,128)} custom-call(f32[64,16,128]{2,1,0:T(8,128)S(1)} %all_to_all.9.parts_ref), custom_call_target="tpu_custom_call" | custom-call | tf_op jit(solution)/shard_map/pallas_call | solution.py:114
Async XLA Ops:
  0.0 5.1 %collective-permute-start = (bf16[32,1024]{1,0:T(8,128)(2,1)}, bf16[32,1024]{1,0:T(8,128)(2,1)S(1)}, u32[]{:S(2)}, u32[]{:S(2)}) collective-permute-start(bf16[32,1024]{1,0:T(8,128)(2,1)} %bitcast.3), channel_id=1, source_target_pairs={{0,128},{128,0},{1,129},{129,1},{2,130},{130,2},{3,131},{131,3},{4... | collective-permute-start | bytes 196616 | tf_op jit(solution)/shard_map/ppermute | solution.py:87
  1.6 3.5 %copy-start = (bf16[1024,32]{0,1:T(8,128)(2,1)S(1)}, bf16[1024,32]{0,1:T(8,128)(2,1)}, u32[]{:S(2)}) copy-start(bf16[1024,32]{0,1:T(8,128)(2,1)} %param.3) | copy-start | bytes 196612
  6.4 2.0 %collective-permute-start.1 = (f32[1024,128]{1,0:T(8,128)S(1)}, f32[1024,128]{1,0:T(8,128)S(1)}, u32[]{:S(2)}, u32[]{:S(2)}) collective-permute-start(f32[1024,128]{1,0:T(8,128)S(1)} %get-tuple-element.8), channel_id=1, source_target_pairs={{0,1},{1,0},{2,3},{3,2},{4,5},{5,4},{6,7},{7,6},{8,9},{9,8},{10,11... | collective-permute-start | bytes 1572872 | tf_op jit(solution)/shard_map/ppermute | solution.py:109

commit v3 on v2

--- a/solution.py
+++ b/solution.py
@@ -10,6 +10,7 @@
 PLANES = 8
 CHIPS = 64
 LANES = 128
+SCALE = 64.0
 
 
 def load_kernel(slab_ref, held_ref, sems):
@@ -74,7 +75,7 @@
 
 def total_kernel(parts_ref, out_ref):
     half, lanes = parts_ref.shape[1:]
-    total = jnp.sum(parts_ref[...], axis=0)
+    total = jnp.sum(parts_ref[...], axis=0) * (1.0 / SCALE)
     out_ref[0:half, :] = total[:, 0 : lanes // 2]
     out_ref[half:, :] = total[:, lanes // 2 :]
 
@@ -106,16 +107,16 @@
         cost_estimate=cost,
     )(held, weights)
     pairs = [(i, i ^ 1) for i in range(2 * CHIPS)]
-    mine = mine + lax.ppermute(other, "col", pairs)
+    mine = (mine + lax.ppermute(other, "col", pairs)) * SCALE
     across = CHIPS // PLANES
     order = [xy * PLANES + z for z in range(PLANES) for xy in range(across)]
     groups = [[2 * chip + core for chip in order] for core in range(2)]
-    parts = lax.all_to_all(mine, "col", 0, 0, axis_index_groups=groups, tiled=True)
+    parts = lax.all_to_all(mine.astype(jnp.float16), "col", 0, 0, axis_index_groups=groups, tiled=True)
     return pl.pallas_call(
         total_kernel,
         out_shape=jax.ShapeDtypeStruct((2 * half, LANES // 2), jnp.float32),
         compiler_params=pltpu.CompilerParams(vmem_limit_bytes=4 * 2**20),
-    )(parts.reshape(CHIPS, half, LANES))
+    )(parts.astype(jnp.float32).reshape(CHIPS, half, LANES))
 
 
 def solution(mesh):

time: 42.5 us -> 37.2 us (0.88)
  blocking collectives: 32.6 us -> 27.5 us
    all_to_all x1, blocking collectives: 32.6 us -> 27.5 us  [shards(): lax.all_to_all(mine.astype(jnp.float16), 'col', 0, 0, axis_index_groups=g...]
  transfers between devices with their start and end apart: 2 -> 2, of which waited for: 1 -> 1; matrix products, arithmetic and copies ran while one was open for 0% -> 0% of each run, Pallas kernels for 11% -> 13%
where the time goes in v3:
time: 37.2 us; the launch traced here: 36.8 us
  blocking collectives  27.5 us (74%)
  Pallas kernels  6.76 us (18%)
  starting transfers between devices  1.67 us (4%)
  waiting for transfers between devices  0.64 us (2%)
    all_to_all x1, blocking collectives, shards(): lax.all_to_all(mine.astype(jnp.float16), 'col', 0, 0, axis_index_groups=g...  27.5 us
    pallas_call x1, Pallas kernels, load(): pl.pallas_call(load_kernel, in_specs=[pl.BlockSpec(memory_space=pltpu.HBM...  3.5 us
    ppermute x1, starting transfers between devices, shards(): far = lax.ppermute(near, 'row', [(0, 1), (1, 0)])  1.58 us
    pallas_call x1, Pallas kernels, shards(): pl.pallas_call(first_kernel, in_specs=[VM] * 3, out_specs=[VM, VM], out_s...  1.27 us
    pallas_call x1, Pallas kernels, shards(): pl.pallas_call(second_kernel, in_specs=[VM] * 2, out_specs=VM, out_shape=...  1.25 us
    pallas_call x1, Pallas kernels, shards(): pl.pallas_call(total_kernel, out_shape=jax.ShapeDtypeStruct((2 * half, LA...  0.75 us
  transfers between devices with their start and end apart: 2, of which 1 were waited for; matrix products, arithmetic and copies ran while one was open for 0% of the time, Pallas kernels for 13%

profile of v3, /device:TPU:4, one launch (start us, length us, event | category | flops | bytes accessed | tf_op | source)
XLA Modules:
  0.0 36.8 jit_solution(5799679588280561839)
XLA Ops:
  0.0 1.6 %collective-permute-start = (bf16[32,1024]{1,0:T(8,128)(2,1)}, bf16[32,1024]{1,0:T(8,128)(2,1)S(1)}, u32[]{:S(2)}, u32[]{:S(2)}) collective-permute-start(bf16[32,1024]{1,0:T(8,128)(2,1)} %bitcast.3), channel_id=1, source_target_pairs={{0,128},{128,0},{1,129},{129,1},{2,130},{130,2},{3,131},{131,3},{4... | collective-permute-start | bytes 196616 | tf_op jit(solution)/shard_map/ppermute | solution.py:88
  1.6 0.0 copy-start
  1.6 3.5 %shard_map.28.slab_ref = bf16[8,8,2,2,16,1024]{5,4,3,2,1,0:T(8,128)(2,1)S(1)} custom-call(bf16[8,8,2,2,16,1024]{5,4,3,2,1,0:T(8,128)(2,1)} %bitcast.5), custom_call_target="tpu_custom_call" | custom-call | bytes 16777216 | tf_op jit(solution)/shard_map/pallas_call | solution.py:28
  5.1 0.0 collective-permute-done.far_ref
  5.1 0.0 copy-done
  5.1 1.3 %shard_map.29 = (f32[1024,128]{1,0:T(8,128)S(1)}, bf16[2,128,1024]{2,1,0:T(8,128)(2,1)S(1)}) custom-call(bf16[8,8,2,2,16,1024]{5,4,3,2,1,0:T(8,128)(2,1)S(1)} %shard_map.28.slab_ref, bf16[32,1024]{1,0:T(8,128)(2,1)S(1)} %bitcast.4, bf16[32,1024]{1,0:T(8,128)(2,1)S(1)} %collective-permute-done.far_ref), custom_call_target="tpu_custom_call" | custom-call | flops 268435456 | bytes 4194304 | tf_op jit(solution)/shard_map/pallas_call | solution.py:93
  6.4 0.1 collective-permute-start.1
  6.5 1.2 %shard_map.30 = f32[1024,128]{1,0:T(8,128)S(1)} custom-call(bf16[8,8,2,2,16,1024]{5,4,3,2,1,0:T(8,128)(2,1)S(1)} %shard_map.28.slab_ref, bf16[2,128,1024]{2,1,0:T(8,128)(2,1)S(1)} %get-tuple-element.7.weights), custom_call_target="tpu_custom_call" | custom-call | flops 268435456 | bytes 4194304 | tf_op jit(solution)/shard_map/pallas_call | solution.py:101
  7.7 0.6 %collective-permute-done.1 = f32[1024,128]{1,0:T(8,128)S(1)} collective-permute-done((f32[1024,128]{1,0:T(8,128)S(1)}, f32[1024,128]{1,0:T(8,128)S(1)}, u32[]{:S(2)}, u32[]{:S(2)}) %collective-permute-start.1) | collective-permute-done | bytes 524320 | tf_op jit(solution)/shard_map/ppermute | solution.py:110
  8.4 0.1 multiply_convert_fusion
  8.4 27.5 %all_to_all.9 = f16[64,16,128]{2,1,0:T(8,128)(2,1)S(1)} all-to-all(f16[64,16,128]{2,1,0:T(8,128)(2,1)S(1)} %bitcast.6), channel_id=1, replica_groups={{0,16,32,48,64,80,96,112,2,18,34,50,66,82,98,114,4,20,36,52,68,84,100,1..., dimensions={0} | all-to-all | bytes 524288 | tf_op jit(solution)/shard_map/all_to_all | solution.py:114
  36.0 0.8 %shard_map.31 = f32[32,64]{1,0:T(8,128)} custom-call(f32[64,16,128]{2,1,0:T(8,128)S(1)} %convert_element_type.8.parts_ref), custom_call_target="tpu_custom_call" | custom-call | tf_op jit(solution)/shard_map/pallas_call | solution.py:115
  (1 shorter events, 0.0 us)
Async XLA Ops:
  0.0 5.1 %collective-permute-start = (bf16[32,1024]{1,0:T(8,128)(2,1)}, bf16[32,1024]{1,0:T(8,128)(2,1)S(1)}, u32[]{:S(2)}, u32[]{:S(2)}) collective-permute-start(bf16[32,1024]{1,0:T(8,128)(2,1)} %bitcast.3), channel_id=1, source_target_pairs={{0,128},{128,0},{1,129},{129,1},{2,130},{130,2},{3,131},{131,3},{4... | collective-permute-start | bytes 196616 | tf_op jit(solution)/shard_map/ppermute | solution.py:88
  1.6 3.5 %copy-start = (bf16[1024,32]{0,1:T(8,128)(2,1)S(1)}, bf16[1024,32]{0,1:T(8,128)(2,1)}, u32[]{:S(2)}) copy-start(bf16[1024,32]{0,1:T(8,128)(2,1)} %param.3) | copy-start | bytes 196612
  6.4 2.0 %collective-permute-start.1 = (f32[1024,128]{1,0:T(8,128)S(1)}, f32[1024,128]{1,0:T(8,128)S(1)}, u32[]{:S(2)}, u32[]{:S(2)}) collective-permute-start(f32[1024,128]{1,0:T(8,128)S(1)} %get-tuple-element.8), channel_id=1, source_target_pairs={{0,1},{1,0},{2,3},{3,2},{4,5},{5,4},{6,7},{7,6},{8,9},{9,8},{10,11... | collective-permute-start | bytes 1572872 | tf_op jit(solution)/shard_map/ppermute | solution.py:110

commit v4 on v3

--- a/solution.py
+++ b/solution.py
@@ -11,6 +11,7 @@
 CHIPS = 64
 LANES = 128
 SCALE = 64.0
+FIRST = 5
 
 
 def load_kernel(slab_ref, held_ref, sems):
@@ -36,6 +37,10 @@
     )(slab)
 
 
+def turned(count):
+    return [(FIRST + step) % count for step in range(count)]
+
+
 def fill(weights, near_ref, far_ref):
     nvec = near_ref.shape[0]
     row = lax.axis_index("row")
@@ -54,7 +59,11 @@
     total = None
     for part in range(2):
         rows = jnp.concatenate(
-            [slab_ref[:, z, which, part].reshape(-1, depth) for z in range(planes)]
+            [
+                slab_ref[at, z, which, part].reshape(-1, depth)
+                for z in turned(planes)
+                for at in (slice(FIRST, None), slice(0, FIRST))
+            ]
         )
         term = lax.dot_general(rows, weights[part], contract, preferred_element_type=jnp.float32)
         total = term if total is None else total + term
@@ -109,7 +118,7 @@
     pairs = [(i, i ^ 1) for i in range(2 * CHIPS)]
     mine = (mine + lax.ppermute(other, "col", pairs)) * SCALE
     across = CHIPS // PLANES
-    order = [xy * PLANES + z for z in range(PLANES) for xy in range(across)]
+    order = [place * PLANES + z for z in turned(PLANES) for place in turned(across)]
     groups = [[2 * chip + core for chip in order] for core in range(2)]
     parts = lax.all_to_all(mine.astype(jnp.float16), "col", 0, 0, axis_index_groups=groups, tiled=True)
     return pl.pallas_call(

time: 37.2 us -> 32.1 us (0.86)
  blocking collectives: 27.5 us -> 22.7 us
    all_to_all x1, blocking collectives: 27.5 us -> 22.7 us  [shards(): lax.all_to_all(mine.astype(jnp.float16), 'col', 0, 0, axis_index_groups=g...]
  transfers between devices with their start and end apart: 2 -> 2, of which waited for: 1 -> 1; matrix products, arithmetic and copies ran while one was open for 0% -> 0% of each run, Pallas kernels for 13% -> 15%
where the time goes in v4:
time: 32.1 us; the launch traced here: 32 us
  blocking collectives  22.7 us (71%)
  Pallas kernels  6.76 us (21%)
  starting transfers between devices  1.67 us (5%)
  waiting for transfers between devices  0.64 us (2%)
    all_to_all x1, blocking collectives, shards(): lax.all_to_all(mine.astype(jnp.float16), 'col', 0, 0, axis_index_groups=g...  22.7 us
    pallas_call x1, Pallas kernels, load(): pl.pallas_call(load_kernel, in_specs=[pl.BlockSpec(memory_space=pltpu.HBM...  3.5 us
    ppermute x1, starting transfers between devices, shards(): far = lax.ppermute(near, 'row', [(0, 1), (1, 0)])  1.58 us
    pallas_call x1, Pallas kernels, shards(): pl.pallas_call(first_kernel, in_specs=[VM] * 3, out_specs=[VM, VM], out_s...  1.27 us
    pallas_call x1, Pallas kernels, shards(): pl.pallas_call(second_kernel, in_specs=[VM] * 2, out_specs=VM, out_shape=...  1.25 us
    pallas_call x1, Pallas kernels, shards(): pl.pallas_call(total_kernel, out_shape=jax.ShapeDtypeStruct((2 * half, LA...  0.75 us
  transfers between devices with their start and end apart: 2, of which 1 were waited for; matrix products, arithmetic and copies ran while one was open for 0% of the time, Pallas kernels for 15%

profile of v4, /device:TPU:4, one launch (start us, length us, event | category | flops | bytes accessed | tf_op | source)
XLA Modules:
  0.0 32.0 jit_solution(16746733209669108901)
XLA Ops:
  0.0 1.6 %collective-permute-start = (bf16[32,1024]{1,0:T(8,128)(2,1)}, bf16[32,1024]{1,0:T(8,128)(2,1)S(1)}, u32[]{:S(2)}, u32[]{:S(2)}) collective-permute-start(bf16[32,1024]{1,0:T(8,128)(2,1)} %bitcast.3), channel_id=1, source_target_pairs={{0,128},{128,0},{1,129},{129,1},{2,130},{130,2},{3,131},{131,3},{4... | collective-permute-start | bytes 196616 | tf_op jit(solution)/shard_map/ppermute | solution.py:97
  1.6 0.0 copy-start
  1.6 3.5 %shard_map.28.slab_ref = bf16[8,8,2,2,16,1024]{5,4,3,2,1,0:T(8,128)(2,1)S(1)} custom-call(bf16[8,8,2,2,16,1024]{5,4,3,2,1,0:T(8,128)(2,1)} %bitcast.5), custom_call_target="tpu_custom_call" | custom-call | bytes 16777216 | tf_op jit(solution)/shard_map/pallas_call | solution.py:29
  5.1 0.0 collective-permute-done.far_ref
  5.1 0.0 copy-done
  5.1 1.3 %shard_map.29 = (f32[1024,128]{1,0:T(8,128)S(1)}, bf16[2,128,1024]{2,1,0:T(8,128)(2,1)S(1)}) custom-call(bf16[8,8,2,2,16,1024]{5,4,3,2,1,0:T(8,128)(2,1)S(1)} %shard_map.28.slab_ref, bf16[32,1024]{1,0:T(8,128)(2,1)S(1)} %bitcast.4, bf16[32,1024]{1,0:T(8,128)(2,1)S(1)} %collective-permute-done.far_ref), custom_call_target="tpu_custom_call" | custom-call | flops 268435456 | bytes 4194304 | tf_op jit(solution)/shard_map/pallas_call | solution.py:102
  6.4 0.1 collective-permute-start.1
  6.5 1.2 %shard_map.30 = f32[1024,128]{1,0:T(8,128)S(1)} custom-call(bf16[8,8,2,2,16,1024]{5,4,3,2,1,0:T(8,128)(2,1)S(1)} %shard_map.28.slab_ref, bf16[2,128,1024]{2,1,0:T(8,128)(2,1)S(1)} %get-tuple-element.7.weights), custom_call_target="tpu_custom_call" | custom-call | flops 268435456 | bytes 4194304 | tf_op jit(solution)/shard_map/pallas_call | solution.py:110
  7.7 0.6 %collective-permute-done.1 = f32[1024,128]{1,0:T(8,128)S(1)} collective-permute-done((f32[1024,128]{1,0:T(8,128)S(1)}, f32[1024,128]{1,0:T(8,128)S(1)}, u32[]{:S(2)}, u32[]{:S(2)}) %collective-permute-start.1) | collective-permute-done | bytes 524320 | tf_op jit(solution)/shard_map/ppermute | solution.py:119
  8.4 0.1 multiply_convert_fusion
  8.4 22.7 %all_to_all.9 = f16[64,16,128]{2,1,0:T(8,128)(2,1)S(1)} all-to-all(f16[64,16,128]{2,1,0:T(8,128)(2,1)S(1)} %bitcast.6), channel_id=1, replica_groups={{90,106,122,10,26,42,58,74,92,108,124,12,28,44,60,76,94,110,126,14,30,4..., dimensions={0} | all-to-all | bytes 524288 | tf_op jit(solution)/shard_map/all_to_all | solution.py:123
  31.2 0.8 %shard_map.31 = f32[32,64]{1,0:T(8,128)} custom-call(f32[64,16,128]{2,1,0:T(8,128)S(1)} %convert_element_type.8.parts_ref), custom_call_target="tpu_custom_call" | custom-call | tf_op jit(solution)/shard_map/pallas_call | solution.py:124
  (1 shorter events, 0.0 us)
Async XLA Ops:
  0.0 5.1 %collective-permute-start = (bf16[32,1024]{1,0:T(8,128)(2,1)}, bf16[32,1024]{1,0:T(8,128)(2,1)S(1)}, u32[]{:S(2)}, u32[]{:S(2)}) collective-permute-start(bf16[32,1024]{1,0:T(8,128)(2,1)} %bitcast.3), channel_id=1, source_target_pairs={{0,128},{128,0},{1,129},{129,1},{2,130},{130,2},{3,131},{131,3},{4... | collective-permute-start | bytes 196616 | tf_op jit(solution)/shard_map/ppermute | solution.py:97
  1.6 3.5 %copy-start = (bf16[1024,32]{0,1:T(8,128)(2,1)S(1)}, bf16[1024,32]{0,1:T(8,128)(2,1)}, u32[]{:S(2)}) copy-start(bf16[1024,32]{0,1:T(8,128)(2,1)} %param.3) | copy-start | bytes 196612
  6.4 2.0 %collective-permute-start.1 = (f32[1024,128]{1,0:T(8,128)S(1)}, f32[1024,128]{1,0:T(8,128)S(1)}, u32[]{:S(2)}, u32[]{:S(2)}) collective-permute-start(f32[1024,128]{1,0:T(8,128)S(1)} %get-tuple-element.8), channel_id=1, source_target_pairs={{0,1},{1,0},{2,3},{3,2},{4,5},{5,4},{6,7},{7,6},{8,9},{9,8},{10,11... | collective-permute-start | bytes 1572872 | tf_op jit(solution)/shard_map/ppermute | solution.py:119

commit v5 on v4

--- a/solution.py
+++ b/solution.py
@@ -10,7 +10,6 @@
 PLANES = 8
 CHIPS = 64
 LANES = 128
-SCALE = 64.0
 FIRST = 5
 
 
@@ -54,14 +53,14 @@
 
 
 def multiply(slab_ref, which, weights, out_ref):
-    planes, half, depth = slab_ref.shape[1], slab_ref.shape[4], slab_ref.shape[5]
+    places, depth = slab_ref.shape[0], slab_ref.shape[5]
     contract = (((1,), (1,)), ((), ()))
     total = None
     for part in range(2):
         rows = jnp.concatenate(
             [
-                slab_ref[at, z, which, part].reshape(-1, depth)
-                for z in turned(planes)
+                slab_ref[place, at, which, part].reshape(-1, depth)
+                for place in turned(places)
                 for at in (slice(FIRST, None), slice(0, FIRST))
             ]
         )
@@ -84,7 +83,7 @@
 
 def total_kernel(parts_ref, out_ref):
     half, lanes = parts_ref.shape[1:]
-    total = jnp.sum(parts_ref[...], axis=0) * (1.0 / SCALE)
+    total = jnp.sum(parts_ref[...], axis=0)
     out_ref[0:half, :] = total[:, 0 : lanes // 2]
     out_ref[half:, :] = total[:, lanes // 2 :]
 
@@ -116,16 +115,30 @@
         cost_estimate=cost,
     )(held, weights)
     pairs = [(i, i ^ 1) for i in range(2 * CHIPS)]
-    mine = (mine + lax.ppermute(other, "col", pairs)) * SCALE
+    mine = mine + lax.ppermute(other, "col", pairs)
     across = CHIPS // PLANES
-    order = [place * PLANES + z for z in turned(PLANES) for place in turned(across)]
-    groups = [[2 * chip + core for chip in order] for core in range(2)]
-    parts = lax.all_to_all(mine.astype(jnp.float16), "col", 0, 0, axis_index_groups=groups, tiled=True)
+
+    def device(place, z, core):
+        return 2 * (place * PLANES + z) + core
+
+    plane = [
+        [device(place, z, core) for place in turned(across)]
+        for z in range(PLANES)
+        for core in range(2)
+    ]
+    line = [
+        [device(place, z, core) for z in turned(PLANES)]
+        for place in range(across)
+        for core in range(2)
+    ]
+    parts = lax.all_to_all(mine, "col", 0, 0, axis_index_groups=plane, tiled=True)
+    held = jnp.sum(parts.reshape(across, PLANES * half, LANES), axis=0)
+    parts = lax.all_to_all(held, "col", 0, 0, axis_index_groups=line, tiled=True)
     return pl.pallas_call(
         total_kernel,
         out_shape=jax.ShapeDtypeStruct((2 * half, LANES // 2), jnp.float32),
         compiler_params=pltpu.CompilerParams(vmem_limit_bytes=4 * 2**20),
-    )(parts.astype(jnp.float32).reshape(CHIPS, half, LANES))
+    )(parts.reshape(PLANES, half, LANES))
 
 
 def solution(mesh):

time: 32.1 us -> 37.1 us (1.16)
  blocking collectives: 22.7 us -> 27.8 us
    all_to_all x1 -> x2, blocking collectives: 22.7 us -> 27.8 us  [the longest x1 14.9 us: shards(): lax.all_to_all(mine, 'col', 0, 0, axis_index_groups=plane, tiled=True)]
  transfers between devices with their start and end apart: 2 -> 2, of which waited for: 1 -> 1; matrix products, arithmetic and copies ran while one was open for 0% -> 0% of each run, Pallas kernels for 15% -> 13%
where the time goes in v5:
time: 37.1 us; the launch traced here: 37 us
  blocking collectives  27.8 us (75%)
  Pallas kernels  6.7 us (18%)
  starting transfers between devices  1.67 us (5%)
  waiting for transfers between devices  0.64 us (2%)
    all_to_all x1, blocking collectives, shards(): lax.all_to_all(mine, 'col', 0, 0, axis_index_groups=plane, tiled=True)  14.9 us
    all_to_all x1, blocking collectives, shards(): lax.all_to_all(held, 'col', 0, 0, axis_index_groups=line, tiled=True)  12.9 us
    pallas_call x1, Pallas kernels, load(): pl.pallas_call(load_kernel, in_specs=[pl.BlockSpec(memory_space=pltpu.HBM...  3.5 us
    ppermute x1, starting transfers between devices, shards(): far = lax.ppermute(near, 'row', [(0, 1), (1, 0)])  1.58 us
    pallas_call x1, Pallas kernels, shards(): pl.pallas_call(first_kernel, in_specs=[VM] * 3, out_specs=[VM, VM], out_s...  1.27 us
    pallas_call x1, Pallas kernels, shards(): pl.pallas_call(second_kernel, in_specs=[VM] * 2, out_specs=VM, out_shape=...  1.25 us
  transfers between devices with their start and end apart: 2, of which 1 were waited for; matrix products, arithmetic and copies ran while one was open for 0% of the time, Pallas kernels for 13%

profile of v5, /device:TPU:4, one launch (start us, length us, event | category | flops | bytes accessed | tf_op | source)
XLA Modules:
  0.0 37.0 jit_solution(12736716897977687890)
XLA Ops:
  0.0 1.6 %collective-permute-start = (bf16[32,1024]{1,0:T(8,128)(2,1)}, bf16[32,1024]{1,0:T(8,128)(2,1)S(1)}, u32[]{:S(2)}, u32[]{:S(2)}) collective-permute-start(bf16[32,1024]{1,0:T(8,128)(2,1)} %bitcast.4), channel_id=1, source_target_pairs={{0,128},{128,0},{1,129},{129,1},{2,130},{130,2},{3,131},{131,3},{4... | collective-permute-start | bytes 196616 | tf_op jit(solution)/shard_map/ppermute | solution.py:96
  1.6 0.0 copy-start
  1.6 3.5 %shard_map.28.slab_ref = bf16[8,8,2,2,16,1024]{5,4,3,2,1,0:T(8,128)(2,1)S(1)} custom-call(bf16[8,8,2,2,16,1024]{5,4,3,2,1,0:T(8,128)(2,1)} %bitcast.6), custom_call_target="tpu_custom_call" | custom-call | bytes 16777216 | tf_op jit(solution)/shard_map/pallas_call | solution.py:28
  5.1 0.0 collective-permute-done.far_ref
  5.1 0.0 copy-done
  5.1 1.3 %shard_map.29 = (f32[1024,128]{1,0:T(8,128)S(1)}, bf16[2,128,1024]{2,1,0:T(8,128)(2,1)S(1)}) custom-call(bf16[8,8,2,2,16,1024]{5,4,3,2,1,0:T(8,128)(2,1)S(1)} %shard_map.28.slab_ref, bf16[32,1024]{1,0:T(8,128)(2,1)S(1)} %bitcast.5, bf16[32,1024]{1,0:T(8,128)(2,1)S(1)} %collective-permute-done.far_ref), custom_call_target="tpu_custom_call" | custom-call | flops 268435456 | bytes 4194304 | tf_op jit(solution)/shard_map/pallas_call | solution.py:101
  6.4 0.1 collective-permute-start.1
  6.5 1.2 %shard_map.30 = f32[1024,128]{1,0:T(8,128)S(1)} custom-call(bf16[8,8,2,2,16,1024]{5,4,3,2,1,0:T(8,128)(2,1)S(1)} %shard_map.28.slab_ref, bf16[2,128,1024]{2,1,0:T(8,128)(2,1)S(1)} %get-tuple-element.7.weights), custom_call_target="tpu_custom_call" | custom-call | flops 268435456 | bytes 4194304 | tf_op jit(solution)/shard_map/pallas_call | solution.py:109
  7.7 0.6 %collective-permute-done.1 = f32[1024,128]{1,0:T(8,128)S(1)} collective-permute-done((f32[1024,128]{1,0:T(8,128)S(1)}, f32[1024,128]{1,0:T(8,128)S(1)}, u32[]{:S(2)}, u32[]{:S(2)}) %collective-permute-start.1) | collective-permute-done | bytes 524320 | tf_op jit(solution)/shard_map/ppermute | solution.py:118
  8.4 0.1 add.3
  8.4 14.9 %all_to_all.18 = f32[8,128,128]{2,1,0:T(8,128)S(1)} all-to-all(f32[8,128,128]{2,1,0:T(8,128)S(1)} %bitcast.7), channel_id=1, replica_groups={{80,96,112,0,16,32,48,64},{81,97,113,1,17,33,49,65},{82,98,114,2,18,34,..., dimensions={0} | all-to-all | bytes 1048576 | tf_op jit(solution)/shard_map/all_to_all | solution.py:134
  23.3 12.9 %all_to_all.19.parts_ref = f32[8,16,128]{2,1,0:T(8,128)S(1)} all-to-all(f32[8,16,128]{2,1,0:T(8,128)S(1)} %bitcast.8), channel_id=1, replica_groups={{10,12,14,0,2,4,6,8},{11,13,15,1,3,5,7,9},{26,28,30,16,18,20,22,24},{27..., dimensions={0} | all-to-all | bytes 131072 | tf_op jit(solution)/shard_map/all_to_all | solution.py:136
  36.3 0.7 %shard_map.31 = f32[32,64]{1,0:T(8,128)} custom-call(f32[8,16,128]{2,1,0:T(8,128)S(1)} %all_to_all.19.parts_ref), custom_call_target="tpu_custom_call" | custom-call | tf_op jit(solution)/shard_map/pallas_call | solution.py:137
  (1 shorter events, 0.0 us)
Async XLA Ops:
  0.0 5.1 %collective-permute-start = (bf16[32,1024]{1,0:T(8,128)(2,1)}, bf16[32,1024]{1,0:T(8,128)(2,1)S(1)}, u32[]{:S(2)}, u32[]{:S(2)}) collective-permute-start(bf16[32,1024]{1,0:T(8,128)(2,1)} %bitcast.4), channel_id=1, source_target_pairs={{0,128},{128,0},{1,129},{129,1},{2,130},{130,2},{3,131},{131,3},{4... | collective-permute-start | bytes 196616 | tf_op jit(solution)/shard_map/ppermute | solution.py:96
  1.6 3.5 %copy-start = (bf16[1024,32]{0,1:T(8,128)(2,1)S(1)}, bf16[1024,32]{0,1:T(8,128)(2,1)}, u32[]{:S(2)}) copy-start(bf16[1024,32]{0,1:T(8,128)(2,1)} %param.3) | copy-start | bytes 196612
  6.4 2.0 %collective-permute-start.1 = (f32[1024,128]{1,0:T(8,128)S(1)}, f32[1024,128]{1,0:T(8,128)S(1)}, u32[]{:S(2)}, u32[]{:S(2)}) collective-permute-start(f32[1024,128]{1,0:T(8,128)S(1)} %get-tuple-element.8), channel_id=1, source_target_pairs={{0,1},{1,0},{2,3},{3,2},{4,5},{5,4},{6,7},{7,6},{8,9},{9,8},{10,11... | collective-permute-start | bytes 1572872 | tf_op jit(solution)/shard_map/ppermute | solution.py:118

commit v6 on v4

--- a/solution.py
+++ b/solution.py
@@ -37,8 +37,8 @@
     )(slab)
 
 
-def turned(count):
-    return [(FIRST + step) % count for step in range(count)]
+def turned(count, first=FIRST):
+    return [(first + step) % count for step in range(count)]
 
 
 def fill(weights, near_ref, far_ref):
@@ -60,8 +60,8 @@
     for part in range(2):
         rows = jnp.concatenate(
             [
-                slab_ref[at, z, which, part].reshape(-1, depth)
-                for z in turned(planes)
+                slab_ref[at, (FIRST - 1 + which + step) & (planes - 1), which, part].reshape(-1, depth)
+                for step in range(planes)
                 for at in (slice(FIRST, None), slice(0, FIRST))
             ]
         )
@@ -118,8 +118,14 @@
     pairs = [(i, i ^ 1) for i in range(2 * CHIPS)]
     mine = (mine + lax.ppermute(other, "col", pairs)) * SCALE
     across = CHIPS // PLANES
-    order = [place * PLANES + z for z in turned(PLANES) for place in turned(across)]
-    groups = [[2 * chip + core for chip in order] for core in range(2)]
+    groups = [
+        [
+            2 * (place * PLANES + z) + core
+            for z in turned(PLANES, FIRST - 1 + core)
+            for place in turned(across)
+        ]
+        for core in range(2)
+    ]
     parts = lax.all_to_all(mine.astype(jnp.float16), "col", 0, 0, axis_index_groups=groups, tiled=True)
     return pl.pallas_call(
         total_kernel,

time: 32.1 us -> 32.1 us (level)
  no operation moved by 1% of the time
where the time goes in v6:
time: 32.1 us; the launch traced here: 32 us
  blocking collectives  22.7 us (71%)
  Pallas kernels  6.76 us (21%)
  starting transfers between devices  1.67 us (5%)
  waiting for transfers between devices  0.65 us (2%)
    all_to_all x1, blocking collectives, shards(): lax.all_to_all(mine.astype(jnp.float16), 'col', 0, 0, axis_index_groups=g...  22.7 us
    pallas_call x1, Pallas kernels, load(): pl.pallas_call(load_kernel, in_specs=[pl.BlockSpec(memory_space=pltpu.HBM...  3.5 us
    ppermute x1, starting transfers between devices, shards(): far = lax.ppermute(near, 'row', [(0, 1), (1, 0)])  1.58 us
    pallas_call x1, Pallas kernels, shards(): pl.pallas_call(first_kernel, in_specs=[VM] * 3, out_specs=[VM, VM], out_s...  1.27 us
    pallas_call x1, Pallas kernels, shards(): pl.pallas_call(second_kernel, in_specs=[VM] * 2, out_specs=VM, out_shape=...  1.25 us
    pallas_call x1, Pallas kernels, shards(): pl.pallas_call(total_kernel, out_shape=jax.ShapeDtypeStruct((2 * half, LA...  0.75 us
    ppermute x1, waiting for transfers between devices, shards(): mine = (mine + lax.ppermute(other, 'col', pairs)) * SCALE  0.64 us
  transfers between devices with their start and end apart: 2, of which 1 were waited for; matrix products, arithmetic and copies ran while one was open for 0% of the time, Pallas kernels for 15%

profile of v6, /device:TPU:4, one launch (start us, length us, event | category | flops | bytes accessed | tf_op | source)
XLA Modules:
  0.0 32.0 jit_solution(2851157520885494488)
XLA Ops:
  0.0 1.6 %collective-permute-start = (bf16[32,1024]{1,0:T(8,128)(2,1)}, bf16[32,1024]{1,0:T(8,128)(2,1)S(1)}, u32[]{:S(2)}, u32[]{:S(2)}) collective-permute-start(bf16[32,1024]{1,0:T(8,128)(2,1)} %bitcast.3), channel_id=1, source_target_pairs={{0,128},{128,0},{1,129},{129,1},{2,130},{130,2},{3,131},{131,3},{4... | collective-permute-start | bytes 196616 | tf_op jit(solution)/shard_map/ppermute | solution.py:97
  1.6 0.0 copy-start
  1.6 3.5 %shard_map.28.slab_ref = bf16[8,8,2,2,16,1024]{5,4,3,2,1,0:T(8,128)(2,1)S(1)} custom-call(bf16[8,8,2,2,16,1024]{5,4,3,2,1,0:T(8,128)(2,1)} %bitcast.5), custom_call_target="tpu_custom_call" | custom-call | bytes 16777216 | tf_op jit(solution)/shard_map/pallas_call | solution.py:29
  5.1 0.0 collective-permute-done.far_ref
  5.1 0.0 copy-done
  5.1 1.3 %shard_map.29 = (f32[1024,128]{1,0:T(8,128)S(1)}, bf16[2,128,1024]{2,1,0:T(8,128)(2,1)S(1)}) custom-call(bf16[8,8,2,2,16,1024]{5,4,3,2,1,0:T(8,128)(2,1)S(1)} %shard_map.28.slab_ref, bf16[32,1024]{1,0:T(8,128)(2,1)S(1)} %bitcast.4, bf16[32,1024]{1,0:T(8,128)(2,1)S(1)} %collective-permute-done.far_ref), custom_call_target="tpu_custom_call" | custom-call | flops 268435456 | bytes 4194304 | tf_op jit(solution)/shard_map/pallas_call | solution.py:102
  6.4 0.1 collective-permute-start.1
  6.5 1.2 %shard_map.30 = f32[1024,128]{1,0:T(8,128)S(1)} custom-call(bf16[8,8,2,2,16,1024]{5,4,3,2,1,0:T(8,128)(2,1)S(1)} %shard_map.28.slab_ref, bf16[2,128,1024]{2,1,0:T(8,128)(2,1)S(1)} %get-tuple-element.7.weights), custom_call_target="tpu_custom_call" | custom-call | flops 268435456 | bytes 4194304 | tf_op jit(solution)/shard_map/pallas_call | solution.py:110
  7.7 0.6 %collective-permute-done.1 = f32[1024,128]{1,0:T(8,128)S(1)} collective-permute-done((f32[1024,128]{1,0:T(8,128)S(1)}, f32[1024,128]{1,0:T(8,128)S(1)}, u32[]{:S(2)}, u32[]{:S(2)}) %collective-permute-start.1) | collective-permute-done | bytes 524320 | tf_op jit(solution)/shard_map/ppermute | solution.py:119
  8.4 0.1 multiply_convert_fusion
  8.5 22.7 %all_to_all.9 = f16[64,16,128]{2,1,0:T(8,128)(2,1)S(1)} all-to-all(f16[64,16,128]{2,1,0:T(8,128)(2,1)S(1)} %bitcast.6), channel_id=1, replica_groups={{88,104,120,8,24,40,56,72,90,106,122,10,26,42,58,74,92,108,124,12,28,44..., dimensions={0} | all-to-all | bytes 524288 | tf_op jit(solution)/shard_map/all_to_all | solution.py:129
  31.2 0.8 %shard_map.31 = f32[32,64]{1,0:T(8,128)} custom-call(f32[64,16,128]{2,1,0:T(8,128)S(1)} %convert_element_type.8.parts_ref), custom_call_target="tpu_custom_call" | custom-call | tf_op jit(solution)/shard_map/pallas_call | solution.py:130
  (1 shorter events, 0.0 us)
Async XLA Ops:
  0.0 5.1 %collective-permute-start = (bf16[32,1024]{1,0:T(8,128)(2,1)}, bf16[32,1024]{1,0:T(8,128)(2,1)S(1)}, u32[]{:S(2)}, u32[]{:S(2)}) collective-permute-start(bf16[32,1024]{1,0:T(8,128)(2,1)} %bitcast.3), channel_id=1, source_target_pairs={{0,128},{128,0},{1,129},{129,1},{2,130},{130,2},{3,131},{131,3},{4... | collective-permute-start | bytes 196616 | tf_op jit(solution)/shard_map/ppermute | solution.py:97
  1.6 3.5 %copy-start = (bf16[1024,32]{0,1:T(8,128)(2,1)S(1)}, bf16[1024,32]{0,1:T(8,128)(2,1)}, u32[]{:S(2)}) copy-start(bf16[1024,32]{0,1:T(8,128)(2,1)} %param.3) | copy-start | bytes 196612
  6.4 2.0 %collective-permute-start.1 = (f32[1024,128]{1,0:T(8,128)S(1)}, f32[1024,128]{1,0:T(8,128)S(1)}, u32[]{:S(2)}, u32[]{:S(2)}) collective-permute-start(f32[1024,128]{1,0:T(8,128)S(1)} %get-tuple-element.8), channel_id=1, source_target_pairs={{0,1},{1,0},{2,3},{3,2},{4,5},{5,4},{6,7},{7,6},{8,9},{9,8},{10,11... | collective-permute-start | bytes 1572872 | tf_op jit(solution)/shard_map/ppermute | solution.py:119

commit v7 on v6

--- a/solution.py
+++ b/solution.py
@@ -42,32 +42,35 @@
 
 
 def fill(weights, near_ref, far_ref):
-    nvec = near_ref.shape[0]
+    nvec, depth = near_ref.shape
     row = lax.axis_index("row")
     near = pl.multiple_of(row * nvec, nvec)
     far = pl.multiple_of((1 - row) * nvec, nvec)
-    zero = jnp.zeros((2 * nvec, weights.shape[2]), weights.dtype)
+    zero = jnp.zeros((2 * nvec, depth), weights.dtype)
     for part in range(2):
-        weights[part, pl.ds(2 * nvec * part + near, nvec), :] = near_ref[...]
-        weights[part, pl.ds(2 * nvec * part + far, nvec), :] = far_ref[...]
-        weights[part, pl.ds(2 * nvec * (1 - part), 2 * nvec), :] = zero
+        columns = slice(part * depth, (part + 1) * depth)
+        weights[pl.ds(2 * nvec * part + near, nvec), columns] = near_ref[...]
+        weights[pl.ds(2 * nvec * part + far, nvec), columns] = far_ref[...]
+        weights[pl.ds(2 * nvec * (1 - part), 2 * nvec), columns] = zero
 
 
 def multiply(slab_ref, which, weights, out_ref):
-    planes, half, depth = slab_ref.shape[1], slab_ref.shape[4], slab_ref.shape[5]
+    planes, depth = slab_ref.shape[1], slab_ref.shape[5]
     contract = (((1,), (1,)), ((), ()))
-    total = None
-    for part in range(2):
-        rows = jnp.concatenate(
-            [
-                slab_ref[at, (FIRST - 1 + which + step) & (planes - 1), which, part].reshape(-1, depth)
-                for step in range(planes)
-                for at in (slice(FIRST, None), slice(0, FIRST))
-            ]
-        )
-        term = lax.dot_general(rows, weights[part], contract, preferred_element_type=jnp.float32)
-        total = term if total is None else total + term
-    out_ref[...] = total
+    rows = jnp.concatenate(
+        [
+            jnp.concatenate(
+                [
+                    slab_ref[at, (FIRST - 1 + which + step) & (planes - 1), which, part].reshape(-1, depth)
+                    for step in range(planes)
+                    for at in (slice(FIRST, None), slice(0, FIRST))
+                ]
+            )
+            for part in range(2)
+        ],
+        axis=1,
+    )
+    out_ref[...] = lax.dot_general(rows, weights[...], contract, preferred_element_type=jnp.float32)
 
 
 def first_kernel(slab_ref, near_ref, far_ref, out_ref, weights):
@@ -103,7 +106,7 @@
         first_kernel,
         in_specs=[VM] * 3,
         out_specs=[VM, VM],
-        out_shape=[product, pltpu.VMEM((2, LANES, depth), slab.dtype)],
+        out_shape=[product, pltpu.VMEM((LANES, 2 * depth), slab.dtype)],
         compiler_params=pltpu.CompilerParams(vmem_limit_bytes=30 * 2**20),
         cost_estimate=cost,
     )(held, near, far)

time: 32.1 us -> 32.1 us (level)
  no operation moved by 1% of the time
where the time goes in v7:
time: 32.1 us; the launch traced here: 32 us
  blocking collectives  22.7 us (71%)
  Pallas kernels  6.77 us (21%)
  starting transfers between devices  1.67 us (5%)
  waiting for transfers between devices  0.64 us (2%)
    all_to_all x1, blocking collectives, shards(): lax.all_to_all(mine.astype(jnp.float16), 'col', 0, 0, axis_index_groups=g...  22.7 us
    pallas_call x1, Pallas kernels, load(): pl.pallas_call(load_kernel, in_specs=[pl.BlockSpec(memory_space=pltpu.HBM...  3.5 us
    ppermute x1, starting transfers between devices, shards(): far = lax.ppermute(near, 'row', [(0, 1), (1, 0)])  1.58 us
    pallas_call x1, Pallas kernels, shards(): pl.pallas_call(first_kernel, in_specs=[VM] * 3, out_specs=[VM, VM], out_s...  1.27 us
    pallas_call x1, Pallas kernels, shards(): pl.pallas_call(second_kernel, in_specs=[VM] * 2, out_specs=VM, out_shape=...  1.25 us
    pallas_call x1, Pallas kernels, shards(): pl.pallas_call(total_kernel, out_shape=jax.ShapeDtypeStruct((2 * half, LA...  0.75 us
    ppermute x1, waiting for transfers between devices, shards(): mine = (mine + lax.ppermute(other, 'col', pairs)) * SCALE  0.64 us
  transfers between devices with their start and end apart: 2, of which 1 were waited for; matrix products, arithmetic and copies ran while one was open for 0% of the time, Pallas kernels for 15%

profile of v7, /device:TPU:4, one launch (start us, length us, event | category | flops | bytes accessed | tf_op | source)
XLA Modules:
  0.0 32.0 jit_solution(9680537457530013977)
XLA Ops:
  0.0 1.6 %collective-permute-start = (bf16[32,1024]{1,0:T(8,128)(2,1)}, bf16[32,1024]{1,0:T(8,128)(2,1)S(1)}, u32[]{:S(2)}, u32[]{:S(2)}) collective-permute-start(bf16[32,1024]{1,0:T(8,128)(2,1)} %bitcast.3), channel_id=1, source_target_pairs={{0,128},{128,0},{1,129},{129,1},{2,130},{130,2},{3,131},{131,3},{4... | collective-permute-start | bytes 196616 | tf_op jit(solution)/shard_map/ppermute | solution.py:100
  1.6 0.0 copy-start
  1.6 3.5 %shard_map.28.slab_ref = bf16[8,8,2,2,16,1024]{5,4,3,2,1,0:T(8,128)(2,1)S(1)} custom-call(bf16[8,8,2,2,16,1024]{5,4,3,2,1,0:T(8,128)(2,1)} %bitcast.5), custom_call_target="tpu_custom_call" | custom-call | bytes 16777216 | tf_op jit(solution)/shard_map/pallas_call | solution.py:29
  5.1 0.0 collective-permute-done.far_ref
  5.1 0.0 copy-done
  5.1 1.3 %shard_map.29 = (f32[1024,128]{1,0:T(8,128)S(1)}, bf16[128,2048]{1,0:T(8,128)(2,1)S(1)}) custom-call(bf16[8,8,2,2,16,1024]{5,4,3,2,1,0:T(8,128)(2,1)S(1)} %shard_map.28.slab_ref, bf16[32,1024]{1,0:T(8,128)(2,1)S(1)} %bitcast.4, bf16[32,1024]{1,0:T(8,128)(2,1)S(1)} %collective-permute-done.far_ref), custom_call_target="tpu_custom_call" | custom-call | flops 268435456 | bytes 4194304 | tf_op jit(solution)/shard_map/pallas_call | solution.py:105
  6.4 0.1 collective-permute-start.1
  6.5 1.2 %shard_map.30 = f32[1024,128]{1,0:T(8,128)S(1)} custom-call(bf16[8,8,2,2,16,1024]{5,4,3,2,1,0:T(8,128)(2,1)S(1)} %shard_map.28.slab_ref, bf16[128,2048]{1,0:T(8,128)(2,1)S(1)} %get-tuple-element.7.weights), custom_call_target="tpu_custom_call" | custom-call | flops 268435456 | bytes 4194304 | tf_op jit(solution)/shard_map/pallas_call | solution.py:113
  7.7 0.6 %collective-permute-done.1 = f32[1024,128]{1,0:T(8,128)S(1)} collective-permute-done((f32[1024,128]{1,0:T(8,128)S(1)}, f32[1024,128]{1,0:T(8,128)S(1)}, u32[]{:S(2)}, u32[]{:S(2)}) %collective-permute-start.1) | collective-permute-done | bytes 524320 | tf_op jit(solution)/shard_map/ppermute | solution.py:122
  8.4 0.1 multiply_convert_fusion
  8.5 22.7 %all_to_all.9 = f16[64,16,128]{2,1,0:T(8,128)(2,1)S(1)} all-to-all(f16[64,16,128]{2,1,0:T(8,128)(2,1)S(1)} %bitcast.6), channel_id=1, replica_groups={{88,104,120,8,24,40,56,72,90,106,122,10,26,42,58,74,92,108,124,12,28,44..., dimensions={0} | all-to-all | bytes 524288 | tf_op jit(solution)/shard_map/all_to_all | solution.py:132
  31.2 0.8 %shard_map.31 = f32[32,64]{1,0:T(8,128)} custom-call(f32[64,16,128]{2,1,0:T(8,128)S(1)} %convert_element_type.8.parts_ref), custom_call_target="tpu_custom_call" | custom-call | tf_op jit(solution)/shard_map/pallas_call | solution.py:133
  (1 shorter events, 0.0 us)
Async XLA Ops:
  0.0 5.1 %collective-permute-start = (bf16[32,1024]{1,0:T(8,128)(2,1)}, bf16[32,1024]{1,0:T(8,128)(2,1)S(1)}, u32[]{:S(2)}, u32[]{:S(2)}) collective-permute-start(bf16[32,1024]{1,0:T(8,128)(2,1)} %bitcast.3), channel_id=1, source_target_pairs={{0,128},{128,0},{1,129},{129,1},{2,130},{130,2},{3,131},{131,3},{4... | collective-permute-start | bytes 196616 | tf_op jit(solution)/shard_map/ppermute | solution.py:100
  1.6 3.5 %copy-start = (bf16[1024,32]{0,1:T(8,128)(2,1)S(1)}, bf16[1024,32]{0,1:T(8,128)(2,1)}, u32[]{:S(2)}) copy-start(bf16[1024,32]{0,1:T(8,128)(2,1)} %param.3) | copy-start | bytes 196612
  6.4 2.0 %collective-permute-start.1 = (f32[1024,128]{1,0:T(8,128)S(1)}, f32[1024,128]{1,0:T(8,128)S(1)}, u32[]{:S(2)}, u32[]{:S(2)}) collective-permute-start(f32[1024,128]{1,0:T(8,128)S(1)} %get-tuple-element.8), channel_id=1, source_target_pairs={{0,1},{1,0},{2,3},{3,2},{4,5},{5,4},{6,7},{7,6},{8,9},{9,8},{10,11... | collective-permute-start | bytes 1572872 | tf_op jit(solution)/shard_map/ppermute | solution.py:122
